TPU v7x, 32 devices: a whole 2x2x4 slice. The times are simulated.
32 devices in a mesh: grp: 2 (over x), blk: 16 (over z, y, core).
Axes of the slice: x: 2, y: 2, z: 4, core: 2. Of those that a mesh axis runs over, the one named last changes fastest.
Arguments:
- feats: bfloat16 [65536, 128], P(('grp', 'blk')), parts along dimension 0, may hold values from -6 to 6
- node_order: int32 [65536], P(('grp', 'blk')), parts along dimension 0, may hold values from 0 to 32767, as said below
- weight: bfloat16 [128, 128], replicated, may hold values from -0.5 to 0.5
- bias: float32 [128], replicated, may hold values from -3 to 3
- block_vals: bfloat16 [10752, 128, 128], P(('grp', 'blk')), parts along dimension 0, may hold values from -0.15625 to 0.15625
- block_rows: int32 [10752], P(('grp', 'blk')), parts along dimension 0, may hold values from 0 to 255, as said below
- block_cols: int32 [10752], P(('grp', 'blk')), parts along dimension 0, may hold values from 0 to 255, as said below
- block_counts: int32 [32], P(('grp', 'blk')), parts along dimension 0, may hold values from 112 to 336, as said below
- cotangent: bfloat16 [65536, 128], P(('grp', 'blk')), parts along dimension 0, may hold values from -6 to 6
Outputs:
- activation: bfloat16 [65536, 128], P(('grp', 'blk')), parts along dimension 0
- grad_feats: bfloat16 [65536, 128], P(('grp', 'blk')), parts along dimension 0
- grad_weight: float32 [256, 128], P('grp'), parts along dimension 0
- grad_bias: float32 [256], P('grp'), parts along dimension 0
There are 2 independent parts, one for each index of `grp`. A program takes and returns all parts, laid end to end along the dimension named above; an argument that names none is the same for every part. Nothing has to cross between parts.
Inputs may be any that keep to these rules, and one draw needn't show every extreme that they name: On every device some permutation maps its own 2048 rows onto themselves: node_order of a device's rows names stored rows of that same device. `block_rows`: slot s of the whole array lies on device s // 336 and names one of that device's own 16 row panels. `block_cols`: slot s names a column panel of a device at most 4 steps from device s // 336 around the closed loop of devices (indices taken modulo the device count). `block_counts`: in every draw some device has exactly 336 live slots.
All inputs are finite; a program needn't handle non-finite values.
Results may differ from a plain program's by a relative error of at most 0.0061.
Values may be sent and summed in bfloat16 or wider, within the bound.
A program may use at most 128 MiB of HBM per device.

v0:
```python
import jax
import jax.numpy as jnp
from jax import lax
from jax.sharding import PartitionSpec as P

REACH = 4


def passed_along(shard, axis, by):
    length = lax.axis_size(axis)
    return lax.ppermute(shard, axis, [(i, (i + by) % length) for i in range(length)])


def on_device(
    feats, node_order, weight, bias, block_vals, block_rows, block_cols, block_counts, cotangent
):
    row_count = feats.shape[0]
    side = block_vals.shape[1]
    width = weight.shape[1]
    panel_count = row_count // side
    slot_count = block_vals.shape[0]
    devices = lax.axis_size("blk")
    me_index = lax.axis_index("blk")
    nodes = feats[node_order - me_index * row_count]
    projected = jnp.dot(nodes, weight, preferred_element_type=jnp.float32).astype(jnp.bfloat16)
    pieces = {0: projected}
    for offset in range(-REACH, REACH + 1):
        if offset != 0:
            pieces[offset] = passed_along(projected, "blk", -offset)
    window = jnp.concatenate([pieces[k] for k in range(-REACH, REACH + 1)], 0).reshape(
        -1, side, width
    )
    local_rows = block_rows - me_index * panel_count
    local_cols = (
        jnp.mod(block_cols // panel_count - me_index + REACH + devices, devices) * panel_count
        + block_cols % panel_count
    )
    slot_ids = jnp.arange(slot_count, dtype=jnp.int32)
    live = slot_ids < block_counts[0]
    masked = jnp.where(live[:, None, None], block_vals, jnp.zeros_like(block_vals))
    prod = jnp.einsum(
        "bij,bjh->bih", masked, window[local_cols], preferred_element_type=jnp.float32
    )
    summed = jnp.zeros((panel_count, side, width), jnp.float32).at[local_rows].add(prod)
    mixed = summed.reshape(row_count, width) + bias
    sig = jax.nn.sigmoid(mixed)
    activation = (mixed * sig).astype(jnp.bfloat16)
    grad_mixed = (cotangent.astype(jnp.float32) * sig * (1.0 + mixed * (1.0 - sig))).astype(
        jnp.bfloat16
    )
    grad_panels = grad_mixed.reshape(panel_count, side, width)
    spread = (2 * REACH + 1) * panel_count
    contrib = jnp.einsum(
        "bji,bjh->bih", masked, grad_panels[local_rows], preferred_element_type=jnp.float32
    )
    partial_grads = jnp.zeros((spread, side, width), jnp.float32).at[local_cols].add(contrib)
    partial_grads = partial_grads.reshape(2 * REACH + 1, row_count, width)
    grad_proj = partial_grads[REACH]
    for offset in range(-REACH, REACH + 1):
        if offset != 0:
            grad_proj = grad_proj + passed_along(partial_grads[offset + REACH], "blk", offset)
    grad_low = grad_proj.astype(jnp.bfloat16)
    weight_term = jnp.dot(nodes.T, grad_low, preferred_element_type=jnp.float32)
    bias_term = jnp.sum(grad_mixed.astype(jnp.float32), axis=0)
    grad_weight, grad_bias = lax.psum((weight_term, bias_term), "blk")
    grad_feats = jnp.dot(grad_low, weight.T, preferred_element_type=jnp.float32).astype(
        jnp.bfloat16
    )
    return (activation, grad_feats, grad_weight, grad_bias)


def solution(mesh):
    in_specs = (
        P(("grp", "blk"), None),
        P(("grp", "blk")),
        P(),
        P(),
        P(("grp", "blk"), None, None),
        P(("grp", "blk")),
        P(("grp", "blk")),
        P(("grp", "blk")),
        P(("grp", "blk"), None),
    )
    out_specs = (P(("grp", "blk"), None), P(("grp", "blk"), None), P("grp", None), P("grp"))
    return jax.shard_map(
        on_device, mesh=mesh, in_specs=in_specs, out_specs=out_specs, check_vma=False
    )
```

profile of v0, /device:TPU:0, one launch (start us, length us, event | category | flops | bytes accessed | tf_op | source)
XLA Modules:
  0.0 518.8 jit_solution(9712924317846431889)
XLA Ops:
  7.2 0.0 copy-start
  7.2 0.0 all-reduce.2.cloned.1.call-start
  7.2 0.8 fusion.10
  8.0 0.2 copy-done
  8.2 6.2 %gather_fusion = bf16[2048,128]{1,0:T(8,128)(2,1)S(1)} fusion(bf16[2048,128]{1,0:T(8,128)(2,1)S(1)} %copy-done, s32[2048]{0:T(1024)S(1)} %fusion.10), kind=kCustom, calls=%fused_computation | custom fusion | bytes 1056768 | tf_op jit(solution)/shard_map/gather | solution.py:24
  14.4 1.0 convolution_convert_fusion.1
  15.5 3.1 collective-permute-start
  18.5 0.7 collective-permute-start.1
  19.2 1.5 collective-permute-start.2
  20.7 0.7 collective-permute-start.3
  21.5 3.7 collective-permute-start.4
  25.2 0.7 compare_select_fusion.1
  26.5 0.7 compare_select_fusion.2
  27.2 6.3 %collective-permute-done = bf16[2048,128]{1,0:T(8,128)(2,1)} collective-permute-done((bf16[2048,128]{1,0:T(8,128)(2,1)S(1)}, bf16[2048,128]{1,0:T(8,128)(2,1)}, u32[]{:S(2)}, u32[]{:S(2)}) %collective-permute-start) | collective-permute-done | bytes 524320 | tf_op jit(solution)/shard_map/ppermute | solution.py:11
  33.5 2.9 collective-permute-start.5
  36.4 1.9 constant_dynamic-update-slice_fusion.8
  38.3 4.6 collective-permute-done.1
  42.9 4.2 collective-permute-start.6
  47.1 0.8 constant_dynamic-update-slice_fusion.7
  47.9 15.7 %collective-permute-done.2 = bf16[2048,128]{1,0:T(8,128)(2,1)S(1)} collective-permute-done((bf16[2048,128]{1,0:T(8,128)(2,1)S(1)}, bf16[2048,128]{1,0:T(8,128)(2,1)S(1)}, u32[]{:S(2)}, u32[]{:S(2)}) %collective-permute-start.2) | collective-permute-done | bytes 524320 | tf_op jit(solution)/shard_map/ppermute | solution.py:11
  63.6 10.8 %collective-permute-start.7 = (bf16[2048,128]{1,0:T(8,128)(2,1)S(1)}, bf16[2048,128]{1,0:T(8,128)(2,1)S(1)}, u32[]{:S(2)}, u32[]{:S(2)}) collective-permute-start(bf16[2048,128]{1,0:T(8,128)(2,1)S(1)} %convolution_convert_fusion.1), channel_id=1, source_target_pairs={{0,12},{1,13},{2,14},{3,15},{4,0},{5,1},{6,2},{7,3},{8,4},{9,5},{1... | collective-permute-start | bytes 1572872 | tf_op jit(solution)/shard_map/ppermute | solution.py:11
  74.4 0.9 constant_dynamic-update-slice_fusion.6
  75.3 0.0 collective-permute-done.3
  75.3 0.8 constant_dynamic-update-slice_fusion.5
  76.1 0.8 constant_dynamic-update-slice_fusion.4
  76.9 0.0 collective-permute-done.4
  76.9 0.8 constant_dynamic-update-slice_fusion.3
  77.8 0.0 collective-permute-done.5
  77.8 0.8 constant_dynamic-update-slice_fusion.2
  78.6 0.8 constant_dynamic-update-slice_fusion.1
  79.4 1.7 collective-permute-done.7
  81.1 0.8 constant_dynamic-update-slice_fusion
  81.9 13.1 %gather_fusion.1 = bf16[336,128,128]{2,1,0:T(8,128)(2,1)} fusion(bf16[144,128,128]{2,1,0:T(8,128)(2,1)} %bitcast.1, s32[1024]{0:T(1024)S(1)} %pad_clamp_fusion.1), kind=kCustom, calls=%fused_computation.1 | custom fusion | bytes 22021440 | tf_op jit(solution)/shard_map/gather | solution.py:42
  95.1 14.2 %fusion.1 = f32[336,128,128]{2,1,0:T(8,128)} fusion(bf16[336,128,128]{2,1,0:T(8,128)(2,1)} %gather_fusion.1, bf16[336,128,128]{2,1,0:T(8,128)(2,1)} %param.13, pred[336]{0:T(512)(128)(4,1)S(1)} %iota_compare_fusion), kind=kOutput, calls=%fused_computation.7 | convolution fusion | flops 1414791168 | bytes 44040528 | tf_op jit(solution)/shard_map/bij,bjh->bih/dot_general | solution.py:41
  109.2 0.1 broadcast_in_dim.30
  109.3 0.0 copy-start.5
  109.3 0.0 copy-start.7
  109.3 44.0 %scatter_fusion = f32[16,128,128]{2,1,0:T(8,128)S(1)} fusion(f32[16,128,128]{2,1,0:T(8,128)S(1)} %broadcast_in_dim.30, s32[336]{0:T(512)S(1)} %compare_select_fusion.2, f32[336,128,128]{2,1,0:T(8,128)} %fusion.1), kind=kCustom, calls=%fused_computation.3 | custom fusion | flops 5505024 | bytes 66061632 | tf_op jit(solution)/shard_map/scatter-add | solution.py:44
  153.3 1.3 convert_reduce_fusion
  154.7 10.7 %gather_fusion.2 = bf16[336,128,128]{2,1,0:T(8,128)(2,1)} fusion(bf16[16,128,128]{2,1,0:T(8,128)(2,1)S(1)} %bitcast.45, s32[1024]{0:T(1024)S(1)} %pad_clamp_fusion), kind=kCustom, calls=%fused_computation.2 | custom fusion | bytes 22021440 | tf_op jit(solution)/shard_map/gather | solution.py:54
  165.4 14.0 %fusion = f32[336,128,128]{2,1,0:T(8,128)} fusion(bf16[336,128,128]{2,1,0:T(8,128)(2,1)} %gather_fusion.2, bf16[336,128,128]{2,1,0:T(8,128)(2,1)} %param.13, pred[336]{0:T(512)(128)(4,1)S(1)} %iota_compare_fusion), kind=kOutput, calls=%fused_computation.6 | convolution fusion | flops 1414791168 | bytes 44040528 | tf_op jit(solution)/shard_map/bji,bjh->bih/dot_general | solution.py:53
  179.4 4.8 broadcast_in_dim.36
  184.2 69.6 %scatter_fusion.1 = f32[144,128,128]{2,1,0:T(8,128)} fusion(f32[144,128,128]{2,1,0:T(8,128)} %broadcast_in_dim.36, s32[336]{0:T(512)S(1)} %compare_select_fusion.1, f32[336,128,128]{2,1,0:T(8,128)} %fusion), kind=kCustom, calls=%fused_computation.4 | custom fusion | flops 5505024 | bytes 66061632 | tf_op jit(solution)/shard_map/scatter-add | solution.py:56
  253.8 6.2 %fusion.19 = (f32[16,128,128]{2,1,0:T(8,128)S(1)}, f32[16,128,128]{2,1,0:T(8,128)}, f32[16,128,128]{2,1,0:T(8,128)}, f32[16,128,128]{2,1,0:T(8,128)}, f32[16,128...) fusion(f32[144,128,128]{2,1,0:T(8,128)} %scatter_fusion.1), kind=kLoop, calls=%fused_computation.57 | loop fusion | bytes 18874368 | tf_op jit(solution)/shard_map/slice | solution.py:58
  260.1 4.5 collective-permute-start.11
  264.6 0.1 collective-permute-start.12
  264.7 1.7 collective-permute-start.13
  266.3 1.7 collective-permute-start.14
  268.0 61.5 %collective-permute-done.10 = f32[2048,128]{1,0:T(8,128)S(1)} collective-permute-done((f32[2048,128]{1,0:T(8,128)S(1)}, f32[2048,128]{1,0:T(8,128)S(1)}, u32[]{:S(2)}, u32[]{:S(2)}) %collective-permute-start.10) | collective-permute-done | bytes 1048608 | tf_op jit(solution)/shard_map/ppermute | solution.py:11
  329.6 0.7 collective-permute-start.15
  330.3 0.0 collective-permute-done.11
  330.3 3.6 collective-permute-start.8
  333.9 0.0 collective-permute-done.12
  333.9 17.2 %collective-permute-start.9 = (f32[2048,128]{1,0:T(8,128)S(1)}, f32[2048,128]{1,0:T(8,128)}, u32[]{:S(2)}, u32[]{:S(2)}) collective-permute-start(f32[2048,128]{1,0:T(8,128)S(1)} %bitcast.46), channel_id=1, source_target_pairs={{0,13},{1,14},{2,15},{3,0},{4,1},{5,2},{6,3},{7,4},{8,5},{9,6},{10... | collective-permute-start | bytes 3145736 | tf_op jit(solution)/shard_map/ppermute | solution.py:11
  351.1 72.6 %psum.15 = f32[128]{0:T(128)} all-reduce(f32[128]{0:T(128)S(1)} %get-tuple-element.4), channel_id=1, replica_groups=mesh['grp'=2,'blk'=16] {'blk'}, use_global_device_ids=true, to_apply=%region_4.5 | all-reduce | flops 128 | bytes 1024 | tf_op jit(solution)/shard_map/psum | solution.py:65
  423.7 0.0 collective-permute-done.13
  423.7 0.0 collective-permute-done.14
  423.7 0.0 collective-permute-done.15
  423.7 3.8 fusion.9
  427.5 1.0 fusion.20
  428.5 0.0 all-reduce.2.cloned.1.call-update
  428.5 1.1 convolution_convert_fusion
  429.6 80.9 %all-reduce.2.cloned.1.call-done = f32[128,128]{1,0:T(8,128)} async-done(((f32[128,128]{1,0:T(8,128)}), f32[128,128]{1,0:T(8,128)}) %all-reduce.2.cloned.1.call-update) | async-done | bytes 65552 | tf_op jit(solution)/shard_map/psum | solution.py:65
  510.5 1.5 copy.27
  (19 shorter events, 0.0 us)
Async XLA Ops:
  7.2 1.1 copy-start
  7.2 503.3 %all-reduce.2.cloned.1.call-start = ((), (), s32[]{:S(2)}) async-start(), calls=%async_computation | async-start | bytes 131072 | tf_op jit(solution)/shard_map/psum | solution.py:65
  15.5 18.1 %collective-permute-start = (bf16[2048,128]{1,0:T(8,128)(2,1)S(1)}, bf16[2048,128]{1,0:T(8,128)(2,1)}, u32[]{:S(2)}, u32[]{:S(2)}) collective-permute-start(bf16[2048,128]{1,0:T(8,128)(2,1)S(1)} %convolution_convert_fusion.1), channel_id=1, source_target_pairs={{0,4},{1,5},{2,6},{3,7},{4,8},{5,9},{6,10},{7,11},{8,12},{9,13},{1... | collective-permute-start | bytes 1572872 | tf_op jit(solution)/shard_map/ppermute | solution.py:11
  18.5 24.4 %collective-permute-start.1 = (bf16[2048,128]{1,0:T(8,128)(2,1)S(1)}, bf16[2048,128]{1,0:T(8,128)(2,1)S(1)}, u32[]{:S(2)}, u32[]{:S(2)}) collective-permute-start(bf16[2048,128]{1,0:T(8,128)(2,1)S(1)} %convolution_convert_fusion.1), channel_id=1, source_target_pairs={{0,3},{1,4},{2,5},{3,6},{4,7},{5,8},{6,9},{7,10},{8,11},{9,12},{10... | collective-permute-start | bytes 1572872 | tf_op jit(solution)/shard_map/ppermute | solution.py:11
  19.2 44.4 %collective-permute-start.2 = (bf16[2048,128]{1,0:T(8,128)(2,1)S(1)}, bf16[2048,128]{1,0:T(8,128)(2,1)S(1)}, u32[]{:S(2)}, u32[]{:S(2)}) collective-permute-start(bf16[2048,128]{1,0:T(8,128)(2,1)S(1)} %convolution_convert_fusion.1), channel_id=1, source_target_pairs={{0,2},{1,3},{2,4},{3,5},{4,6},{5,7},{6,8},{7,9},{8,10},{9,11},{10,... | collective-permute-start | bytes 1572872 | tf_op jit(solution)/shard_map/ppermute | solution.py:11
  20.7 54.5 %collective-permute-start.3 = (bf16[2048,128]{1,0:T(8,128)(2,1)S(1)}, bf16[2048,128]{1,0:T(8,128)(2,1)S(1)}, u32[]{:S(2)}, u32[]{:S(2)}) collective-permute-start(bf16[2048,128]{1,0:T(8,128)(2,1)S(1)} %convolution_convert_fusion.1), channel_id=1, source_target_pairs={{0,1},{1,2},{2,3},{3,4},{4,5},{5,6},{6,7},{7,8},{8,9},{9,10},{10,1... | collective-permute-start | bytes 1572872 | tf_op jit(solution)/shard_map/ppermute | solution.py:11
  21.5 55.5 %collective-permute-start.4 = (bf16[2048,128]{1,0:T(8,128)(2,1)S(1)}, bf16[2048,128]{1,0:T(8,128)(2,1)S(1)}, u32[]{:S(2)}, u32[]{:S(2)}) collective-permute-start(bf16[2048,128]{1,0:T(8,128)(2,1)S(1)} %convolution_convert_fusion.1), channel_id=1, source_target_pairs={{0,15},{1,0},{2,1},{3,2},{4,3},{5,4},{6,5},{7,6},{8,7},{9,8},{10,9... | collective-permute-start | bytes 1572872 | tf_op jit(solution)/shard_map/ppermute | solution.py:11
  33.5 44.3 %collective-permute-start.5 = (bf16[2048,128]{1,0:T(8,128)(2,1)S(1)}, bf16[2048,128]{1,0:T(8,128)(2,1)S(1)}, u32[]{:S(2)}, u32[]{:S(2)}) collective-permute-start(bf16[2048,128]{1,0:T(8,128)(2,1)S(1)} %convolution_convert_fusion.1), channel_id=1, source_target_pairs={{0,14},{1,15},{2,0},{3,1},{4,2},{5,3},{6,4},{7,5},{8,6},{9,7},{10,... | collective-permute-start | bytes 1572872 | tf_op jit(solution)/shard_map/ppermute | solution.py:11
  42.9 35.7 %collective-permute-start.6 = (bf16[2048,128]{1,0:T(8,128)(2,1)S(1)}, bf16[2048,128]{1,0:T(8,128)(2,1)S(1)}, u32[]{:S(2)}, u32[]{:S(2)}) collective-permute-start(bf16[2048,128]{1,0:T(8,128)(2,1)S(1)} %convolution_convert_fusion.1), channel_id=1, source_target_pairs={{0,13},{1,14},{2,15},{3,0},{4,1},{5,2},{6,3},{7,4},{8,5},{9,6},{10... | collective-permute-start | bytes 1572872 | tf_op jit(solution)/shard_map/ppermute | solution.py:11
  63.6 17.5 %collective-permute-start.7 = (bf16[2048,128]{1,0:T(8,128)(2,1)S(1)}, bf16[2048,128]{1,0:T(8,128)(2,1)S(1)}, u32[]{:S(2)}, u32[]{:S(2)}) collective-permute-start(bf16[2048,128]{1,0:T(8,128)(2,1)S(1)} %convolution_convert_fusion.1), channel_id=1, source_target_pairs={{0,12},{1,13},{2,14},{3,15},{4,0},{5,1},{6,2},{7,3},{8,4},{9,5},{1... | collective-permute-start | bytes 1572872 | tf_op jit(solution)/shard_map/ppermute | solution.py:11
  109.3 44.0 %copy-start.5 = (bf16[2048,128]{1,0:T(8,128)(2,1)S(1)}, bf16[2048,128]{1,0:T(8,128)(2,1)}, u32[]{:S(2)}) copy-start(bf16[2048,128]{1,0:T(8,128)(2,1)} %param.17) | copy-start | bytes 1572868
  109.3 44.0 %copy-start.7 = (f32[128]{0:T(128)S(1)}, f32[128]{0:T(128)}, u32[]{:S(2)}) copy-start(f32[128]{0:T(128)} %param.12) | copy-start | bytes 1540
  184.2 327.8 %copy-start.1 = (bf16[2048,128]{1,0:T(8,128)(2,1)S(1)}, bf16[2048,128]{1,0:T(8,128)(2,1)}, u32[]{:S(2)}) copy-start(bf16[2048,128]{1,0:T(8,128)(2,1)} %param.9) | copy-start | bytes 1572868
  253.8 174.7 %copy-start.6 = (bf16[128,128]{1,0:T(8,128)(2,1)S(1)}, bf16[128,128]{1,0:T(8,128)(2,1)}, u32[]{:S(2)}) copy-start(bf16[128,128]{1,0:T(8,128)(2,1)} %param.11) | copy-start | bytes 98308
  260.1 69.5 %collective-permute-start.10 = (f32[2048,128]{1,0:T(8,128)S(1)}, f32[2048,128]{1,0:T(8,128)S(1)}, u32[]{:S(2)}, u32[]{:S(2)}) collective-permute-start(f32[2048,128]{1,0:T(8,128)S(1)} %bitcast.49), channel_id=1, source_target_pairs={{0,14},{1,15},{2,0},{3,1},{4,2},{5,3},{6,4},{7,5},{8,6},{9,7},{10,... | collective-permute-start | bytes 3145736 | tf_op jit(solution)/shard_map/ppermute | solution.py:11
  260.1 70.2 %collective-permute-start.11 = (f32[2048,128]{1,0:T(8,128)S(1)}, f32[2048,128]{1,0:T(8,128)S(1)}, u32[]{:S(2)}, u32[]{:S(2)}) collective-permute-start(f32[2048,128]{1,0:T(8,128)S(1)} %bitcast.48), channel_id=1, source_target_pairs={{0,15},{1,0},{2,1},{3,2},{4,3},{5,4},{6,5},{7,6},{8,7},{9,8},{10,9... | collective-permute-start | bytes 3145736 | tf_op jit(solution)/shard_map/ppermute | solution.py:11
  264.6 69.3 %collective-permute-start.12 = (f32[2048,128]{1,0:T(8,128)S(1)}, f32[2048,128]{1,0:T(8,128)S(1)}, u32[]{:S(2)}, u32[]{:S(2)}) collective-permute-start(f32[2048,128]{1,0:T(8,128)S(1)} %bitcast.47), channel_id=1, source_target_pairs={{0,1},{1,2},{2,3},{3,4},{4,5},{5,6},{6,7},{7,8},{8,9},{9,10},{10,1... | collective-permute-start | bytes 3145736 | tf_op jit(solution)/shard_map/ppermute | solution.py:11
  264.7 159.0 %collective-permute-start.13 = (f32[2048,128]{1,0:T(8,128)}, f32[2048,128]{1,0:T(8,128)}, u32[]{:S(2)}, u32[]{:S(2)}) collective-permute-start(f32[2048,128]{1,0:T(8,128)} %bitcast.10), channel_id=1, source_target_pairs={{0,2},{1,3},{2,4},{3,5},{4,6},{5,7},{6,8},{7,9},{8,10},{9,11},{10,... | collective-permute-start | bytes 3145736 | tf_op jit(solution)/shard_map/ppermute | solution.py:11
  266.3 157.4 %collective-permute-start.14 = (f32[2048,128]{1,0:T(8,128)}, f32[2048,128]{1,0:T(8,128)}, u32[]{:S(2)}, u32[]{:S(2)}) collective-permute-start(f32[2048,128]{1,0:T(8,128)} %bitcast.11), channel_id=1, source_target_pairs={{0,3},{1,4},{2,5},{3,6},{4,7},{5,8},{6,9},{7,10},{8,11},{9,12},{10... | collective-permute-start | bytes 3145736 | tf_op jit(solution)/shard_map/ppermute | solution.py:11
  329.6 21.5 %copy-start.2 = (f32[2048,128]{1,0:T(8,128)}, f32[2048,128]{1,0:T(8,128)S(1)}, u32[]{:S(2)}) copy-start(f32[2048,128]{1,0:T(8,128)S(1)} %collective-permute-done.10) | copy-start | bytes 3145732
  329.6 94.1 %collective-permute-start.15 = (f32[2048,128]{1,0:T(8,128)}, f32[2048,128]{1,0:T(8,128)}, u32[]{:S(2)}, u32[]{:S(2)}) collective-permute-start(f32[2048,128]{1,0:T(8,128)} %bitcast.12), channel_id=1, source_target_pairs={{0,4},{1,5},{2,6},{3,7},{4,8},{5,9},{6,10},{7,11},{8,12},{9,13},{1... | collective-permute-start | bytes 3145736 | tf_op jit(solution)/shard_map/ppermute | solution.py:11
  330.3 20.8 %copy-start.3 = (f32[2048,128]{1,0:T(8,128)}, f32[2048,128]{1,0:T(8,128)S(1)}, u32[]{:S(2)}) copy-start(f32[2048,128]{1,0:T(8,128)S(1)} %collective-permute-done.11) | copy-start | bytes 3145732
  330.3 93.4 %collective-permute-start.8 = (f32[2048,128]{1,0:T(8,128)}, f32[2048,128]{1,0:T(8,128)}, u32[]{:S(2)}, u32[]{:S(2)}) collective-permute-start(f32[2048,128]{1,0:T(8,128)} %bitcast.5), channel_id=1, source_target_pairs={{0,12},{1,13},{2,14},{3,15},{4,0},{5,1},{6,2},{7,3},{8,4},{9,5},{1... | collective-permute-start | bytes 3145736 | tf_op jit(solution)/shard_map/ppermute | solution.py:11
  333.9 17.2 %copy-start.4 = (f32[2048,128]{1,0:T(8,128)}, f32[2048,128]{1,0:T(8,128)S(1)}, u32[]{:S(2)}) copy-start(f32[2048,128]{1,0:T(8,128)S(1)} %collective-permute-done.12) | copy-start | bytes 3145732
  333.9 89.9 %collective-permute-start.9 = (f32[2048,128]{1,0:T(8,128)S(1)}, f32[2048,128]{1,0:T(8,128)}, u32[]{:S(2)}, u32[]{:S(2)}) collective-permute-start(f32[2048,128]{1,0:T(8,128)S(1)} %bitcast.46), channel_id=1, source_target_pairs={{0,13},{1,14},{2,15},{3,0},{4,1},{5,2},{6,3},{7,4},{8,5},{9,6},{10... | collective-permute-start | bytes 3145736 | tf_op jit(solution)/shard_map/ppermute | solution.py:11
Sparse Core Ops, SparseCore 0:
  428.7 81.8 all-reduce.1
where the time goes:
time: 521 us; the launch traced here: 519 us
  waiting for transfers between devices  171 us (33%)
  other arithmetic  121 us (23%)
  blocking collectives  72.6 us (14%)
  starting transfers between devices  57 us (11%)
  local copies, waits for them, and re-layouts  51.5 us (10%)
  matrix products  31.2 us (6%)
  between operations  14.8 us (3%)
    ppermute x16, waiting for transfers between devices, passed_along(): lax.ppermute(shard, axis, [(i, (i + by) % length) for i in range(length)])  89.8 us
    psum x1, waiting for transfers between devices, on_device(): grad_weight, grad_bias = lax.psum((weight_term, bias_term), 'blk')  80.9 us
    psum x1, blocking collectives, on_device(): grad_weight, grad_bias = lax.psum((weight_term, bias_term), 'blk')  72.6 us
    scatter-add x1, other arithmetic, on_device(): jnp.zeros((spread, side, width), jnp.float32).at[local_cols].add(contrib)  69.6 us
    ppermute x16, starting transfers between devices, passed_along(): lax.ppermute(shard, axis, [(i, (i + by) % length) for i in range(length)])  57 us
    scatter-add x1, other arithmetic, on_device(): jnp.zeros((panel_count, side, width), jnp.float32).at[local_rows].add(prod)  44 us
    dot_general x1, matrix products, on_device(): jnp.einsum('bij,bjh->bih', masked, window[local_cols], preferred_element_...  14.2 us
    dot_general x1, matrix products, on_device(): jnp.einsum('bji,bjh->bih', masked, grad_panels[local_rows], preferred_ele...  14 us
  transfers between devices with their start and end apart: 17, of which 6 were waited for; matrix products, arithmetic and copies ran while one was open for 2% of the time, Pallas kernels for 0%

commit v1 on v0

v1 whole, which is shorter than its diff:
```python
import functools

import jax
import jax.numpy as jnp
from jax import lax
from jax.experimental import pallas as pl
from jax.experimental.pallas import tpu as pltpu
from jax.sharding import PartitionSpec as P

QUAD = 4
CHUNKS = 12
UNROLL = 4
BF = jnp.bfloat16
F32 = jnp.float32
MESH = pl.DeviceIdType.MESH
VMEM_LIMIT = 58 * 1024 * 1024


def vmem():
    return pl.BlockSpec(memory_space=pltpu.VMEM)


def smem():
    return pl.BlockSpec(memory_space=pltpu.SMEM)


def gather_kernel(order, feats, weight, nodes, projected, wide, picked):
    count = feats.shape[0]
    wide[...] = feats[...].astype(F32)

    def body(i, carry):
        base = pl.multiple_of(i * 16, 16)
        for u in range(16):
            src = lax.rem(order[base + u], count)
            picked[pl.ds(base + u, 1), :] = wide[pl.ds(src, 1), :]
        return carry

    lax.fori_loop(0, count // 16, body, 0)
    part = 512 if count % 512 == 0 else count

    def product(i, carry):
        at = pl.ds(pl.multiple_of(i * part, part), part)
        rows = picked[at, :].astype(BF)
        nodes[at, :] = rows
        projected[at, :] = jnp.dot(rows, weight[...], preferred_element_type=F32).astype(BF)
        return carry

    lax.fori_loop(0, count // part, product, 0)


def places(n):
    me = lax.axis_index("blk")
    q, j = me // QUAD, me % QUAD
    y, c = j // 2, j % 2
    quads = n // QUAD
    up = ((q + 1) % quads) * QUAD + j
    down = ((q + quads - 1) % quads) * QUAD + j
    across = q * QUAD + (1 - y) * 2 + c
    twin = q * QUAD + y * 2 + (1 - c)
    return me, q, j, y, c, up, down, across, twin


def greet(devices):
    barrier = pltpu.get_barrier_semaphore()
    for device in devices:
        pl.semaphore_signal(
            barrier, inc=1, device_id=(lax.axis_index("grp"), device), device_id_type=MESH
        )
    pl.semaphore_wait(barrier, len(devices))


def send(src, dst, send_sem, recv_sem, device):
    copy = pltpu.make_async_remote_copy(
        src_ref=src,
        dst_ref=dst,
        send_sem=send_sem,
        recv_sem=recv_sem,
        device_id=(lax.axis_index("grp"), device),
        device_id_type=MESH,
    )
    copy.start()
    return copy


def window_kernel(n, own, window, send_sem, recv_sem, local_sem):
    me, q, j, y, c, up, down, across, twin = places(n)
    nj = (1 - y) * 2 + c
    tj = y * 2 + (1 - c)
    fj = (1 - y) * 2 + (1 - c)
    beyond = (1 - y) * up + y * down
    half = own.shape[0] // 2
    greet((up, down, across, twin))
    sent = []

    def piece(slot, p, h):
        return window.at[slot * QUAD + p, pl.ds(h * half, half), :]

    def push(src, slot, p, h, device):
        k = len(sent)
        sent.append(
            send(src, piece(slot, p, h), send_sem.at[k], recv_sem.at[slot * QUAD + p, h], device)
        )

    def arrived(slot, p, h):
        spot = piece(slot, p, h)
        pltpu.make_async_remote_copy(
            src_ref=spot,
            dst_ref=spot,
            send_sem=send_sem.at[0],
            recv_sem=recv_sem.at[slot * QUAD + p, h],
            device_id=(lax.axis_index("grp"), twin),
            device_id_type=MESH,
        ).wait_recv()
        return spot

    for h in (1, 0):
        mine = own.at[pl.ds(h * half, half), :]
        push(mine, 1, j, h, across)
        push(mine, 0, j, h, up)
        push(mine, 2, j, h, down)
        push(mine, 1, j, h, twin)
    keep = pltpu.make_async_copy(own, window.at[QUAD + j], local_sem)
    keep.start()

    spot = arrived(1, nj, 1)
    push(spot, 2 * y, nj, 1, beyond)
    push(spot, 1, nj, 1, twin)
    near, other = 2 * (1 - y), 2 * y
    zs = 2 * (1 - c)
    zo = 2 * c
    for h in (1, 0):
        if h == 0:
            spot = arrived(1, nj, 0)
            push(spot, 1, nj, 0, twin)
        spot = arrived(near, j, h)
        if h == 0:
            push(spot, near, j, 0, across)
        arrived(other, j, h)
        push(piece(zs, j, h), zs, j, h, twin)
    for h in (1, 0):
        spot = arrived(2 * y, nj, h)
        push(spot, 2 * y, nj, h, twin)
    for h in (1, 0):
        arrived(1, tj, h)
        arrived(1, fj, h)
        arrived(zo, tj, h)
        arrived(2 * y, fj, h)
    keep.wait()
    for copy in sent:
        copy.wait_send()


def spmm_kernel(
    counts, rows, cols, window, bias, cotangent, vals_hbm,
    act, partial, grad_bias, vals, acc, flipped, grads, sems,
):
    slots, side, width = vals_hbm.shape
    panels = acc.shape[0] - 1
    spread = grads.shape[0] - 1
    per = slots // CHUNKS
    count = counts[0]

    def fetch(k):
        at = pl.ds(k * per, per)
        return pltpu.make_async_copy(vals_hbm.at[at], vals.at[at], sems.at[k])

    for k in range(CHUNKS):
        @pl.when(k * per < count)
        def _(k=k):
            fetch(k).start()

    acc[...] = jnp.zeros_like(acc)

    def forward(i, carry):
        at = [i * UNROLL + u for u in range(UNROLL)]
        prods = [
            jnp.dot(vals[s], window[cols[s]], preferred_element_type=F32) for s in at
        ]
        for s, prod in zip(at, prods):
            row = jnp.where(s < count, rows[s], panels)
            acc[row] += prod
        return carry

    for k in range(CHUNKS):
        @pl.when(k * per < count)
        def _(k=k):
            fetch(k).wait()
            lax.fori_loop(k * per // UNROLL, (k + 1) * per // UNROLL, forward, 0)

    def clear(p, carry):
        grads[p] = jnp.zeros((side, width), F32)
        return carry

    lax.fori_loop(0, spread, clear, 0)

    def middle(r, total):
        mixed = acc[r] + bias[...]
        sig = 1.0 / (1.0 + jnp.exp(-mixed))
        act[r] = (mixed * sig).astype(BF)
        grad = cotangent[r].astype(F32) * sig * (1.0 + mixed * (1.0 - sig))
        low = grad.astype(BF).astype(F32)
        flipped[r] = low.T.astype(BF)
        return total + jnp.sum(low.reshape(side // 8, 8, width), axis=0)

    grad_bias[...] = lax.fori_loop(0, panels, middle, jnp.zeros((8, width), F32))

    def backward(i, carry):
        at = [i * UNROLL + u for u in range(UNROLL)]
        prods = [
            jnp.dot(flipped[rows[s]], vals[s], preferred_element_type=F32) for s in at
        ]
        for s, prod in zip(at, prods):
            col = jnp.where(s < count, cols[s], spread)
            grads[col] += prod
        return carry

    lax.fori_loop(0, (count + UNROLL - 1) // UNROLL, backward, 0)

    def store(p, carry):
        partial[p] = grads[p].astype(BF)
        return carry

    lax.fori_loop(0, spread, store, 0)


def reduce_kernel(
    n, shared, partial, nodes, weight, grad_bias,
    grad_feats, grad_weight, bias_out,
    from_twin, from_across, from_z, far_across, far_z, mid, work,
    share, gathered, biases, own_bias,
    send_sem, recv_sem, small_send, small_recv,
):
    me, q, j, y, c, up, down, across, twin = places(n)
    nj = (1 - y) * 2 + c
    tj = y * 2 + (1 - c)
    fj = (1 - y) * 2 + (1 - c)
    panels = partial.shape[1]
    half = panels // 2
    if shared:
        greet([(me + d) % n for d in range(1, n)])
    else:
        greet((up, down, across, twin))
    sent = []

    def push(src, dst, key, device):
        k = len(sent)
        copy = send(src, dst, send_sem.at[k], recv_sem.at[key], device)
        sent.append(copy)

    def arrived(dst, key):
        pltpu.make_async_remote_copy(
            src_ref=dst,
            dst_ref=dst,
            send_sem=send_sem.at[0],
            recv_sem=recv_sem.at[key],
            device_id=(lax.axis_index("grp"), twin),
            device_id_type=MESH,
        ).wait_recv()

    def part(ref, index, h):
        return ref.at[index, pl.ds(h * half, half)]

    def merge(dst, a, b):
        def body(p, carry):
            dst[p] = (a[p].astype(F32) + b[p].astype(F32)).astype(BF)
            return carry

        lax.fori_loop(0, half, body, 0)

    order = [
        (0, 2 * y * QUAD + fj),
        (1, QUAD + fj),
        (2, 2 * c * QUAD + tj),
        (3, QUAD + tj),
    ]
    for k, index in order:
        for h in (1, 0):
            push(part(partial, index, h), part(from_twin, k, h), 2 * k + h, twin)
    if shared:
        small = []
        own_bias[...] = grad_bias[...]
        for d in range(1, n):
            small.append(
                send(own_bias, biases.at[me], small_send.at[0, d], small_recv.at[0, me],
                     (me + d) % n)
            )
        biases[me] = grad_bias[...]

    back = (1 - y) * down + y * up
    for h in (1, 0):
        arrived(part(from_twin, 0, h), h)
        merge(part(mid, 0, h), part(partial, 2 * y * QUAD + nj, h), part(from_twin, 0, h))
        if h == 1:
            push(part(mid, 0, 1), far_z, 8, back)
        else:
            push(part(mid, 0, 0), far_across, 9, across)
    near, other = 2 * (1 - y), 2 * y
    zs, zo = 2 * (1 - c), 2 * c
    for h in (1, 0):
        arrived(part(from_twin, 2, h), 4 + h)
        merge(part(mid, 2, h), part(partial, zs * QUAD + j, h), part(from_twin, 2, h))

        def fill(p, carry, h=h):
            mid[1, h * half + p] = partial[zo * QUAD + j, h * half + p]
            return carry

        lax.fori_loop(0, half, fill, 0)
    near_at = 1 + (near == zs).astype(jnp.int32)
    zs_up = (zs == 2).astype(jnp.int32)
    to_zs = zs_up * up + (1 - zs_up) * down
    to_zo = (1 - zs_up) * up + zs_up * down
    push(part(mid, 2, 1), part(from_z, 1 - zs_up, 1), 10 + 2 * (1 - zs_up) + 1, to_zs)
    push(part(mid, 1, 1), part(from_z, zs_up, 1), 10 + 2 * zs_up + 1, to_zo)
    arrived(far_across, 9)
    merge(part(mid, near_at, 0), part(mid, near_at, 0), far_across)
    push(part(mid, 2, 0), part(from_z, 1 - zs_up, 0), 10 + 2 * (1 - zs_up), to_zs)
    push(part(mid, 1, 0), part(from_z, zs_up, 0), 10 + 2 * zs_up, to_zo)
    arrived(part(from_twin, 1, 0), 2)
    merge(part(mid, 3, 0), part(partial, QUAD + nj, 0), part(from_twin, 1, 0))
    push(part(mid, 3, 0), part(from_across, 0, 0), 14, across)
    arrived(part(from_twin, 1, 1), 3)
    merge(part(mid, 3, 1), part(partial, QUAD + nj, 1), part(from_twin, 1, 1))
    arrived(far_z, 8)
    merge(part(mid, 3, 1), part(mid, 3, 1), far_z)
    push(part(mid, 3, 1), part(from_across, 0, 1), 15, across)

    work[...] = jnp.zeros_like(work)
    for h in (0, 1):
        arrived(part(from_twin, 3, h), 6 + h)
        arrived(part(from_z, 0, h), 10 + h)
        arrived(part(from_z, 1, h), 12 + h)
        arrived(part(from_across, 0, h), 14 + h)

        def finish(i, carry, h=h):
            p = h * half + i
            total = partial[QUAD + j, p].astype(F32) + from_twin[3, p].astype(F32)
            total = total + from_across[0, p].astype(F32)
            total = total + from_z[0, p].astype(F32) + from_z[1, p].astype(F32)
            low = total.astype(BF)
            work[...] += jnp.dot(low, nodes[p], preferred_element_type=F32)
            flat = total.T.astype(BF)
            grad_feats[p] = lax.dot_general(
                flat, weight[...], (((1,), (1,)), ((), ())), preferred_element_type=F32
            ).astype(BF)
            return carry

        lax.fori_loop(0, half, finish, 0)

    if shared:
        step = work.shape[0] // n

        def small_wait(dst, level, source):
            pltpu.make_async_remote_copy(
                src_ref=dst,
                dst_ref=dst,
                send_sem=small_send.at[0, 0],
                recv_sem=small_recv.at[level, source],
                device_id=(lax.axis_index("grp"), twin),
                device_id_type=MESH,
            ).wait_recv()

        for d in range(1, n):
            peer = (me + d) % n
            small.append(
                send(work.at[pl.ds(peer * step, step), :], share.at[me],
                     small_send.at[1, d], small_recv.at[1, me], peer)
            )
        share[me] = work[pl.ds(pl.multiple_of(me * step, step), step), :]
        for d in range(1, n):
            small_wait(share.at[(me + d) % n], 1, (me + d) % n)
        gathered[me] = jnp.sum(share[...], axis=0)
        for d in range(1, n):
            small.append(
                send(gathered.at[me], gathered.at[me], small_send.at[2, d],
                     small_recv.at[2, me], (me + d) % n)
            )
        for d in range(1, n):
            small_wait(biases.at[(me + d) % n], 0, (me + d) % n)
        bias_out[...] = jnp.sum(jnp.sum(biases[...], axis=0), axis=0, keepdims=True)
        for d in range(1, n):
            small_wait(gathered.at[(me + d) % n], 2, (me + d) % n)
        grad_weight[...] = gathered[...].reshape(work.shape).T
        for copy in small:
            copy.wait_send()
    else:
        grad_weight[...] = work[...].T
        bias_out[...] = jnp.sum(grad_bias[...], axis=0, keepdims=True)
    for copy in sent:
        copy.wait_send()


def on_device(
    feats, node_order, weight, bias, block_vals, block_rows, block_cols, block_counts, cotangent
):
    row_count, width_in = feats.shape
    slots, side, _ = block_vals.shape
    width = weight.shape[1]
    panels = row_count // side
    n = lax.axis_size("blk")
    quads = n // QUAD
    pieces = 3 * QUAD
    me = lax.axis_index("blk")

    rows = block_rows - me * panels
    owner = block_cols // panels
    slot = jnp.mod(owner // QUAD - me // QUAD + 1 + quads, quads)
    cols = (slot * QUAD + owner % QUAD) * panels + block_cols % panels

    nodes, projected = pl.pallas_call(
        gather_kernel,
        out_shape=(
            jax.ShapeDtypeStruct((row_count, width_in), BF),
            jax.ShapeDtypeStruct((row_count, width), BF),
        ),
        in_specs=[smem(), vmem(), vmem()],
        out_specs=(vmem(), vmem()),
        scratch_shapes=[
            pltpu.VMEM((row_count, width_in), F32),
            pltpu.VMEM((row_count, width_in), F32),
        ],
        compiler_params=pltpu.CompilerParams(vmem_limit_bytes=VMEM_LIMIT),
        name="gather_project",
    )(node_order, feats, weight)

    window = pl.pallas_call(
        functools.partial(window_kernel, n),
        out_shape=jax.ShapeDtypeStruct((pieces, row_count, width), BF),
        in_specs=[vmem()],
        out_specs=vmem(),
        scratch_shapes=[
            pltpu.SemaphoreType.DMA((24,)),
            pltpu.SemaphoreType.DMA((pieces, 2)),
            pltpu.SemaphoreType.DMA,
        ],
        compiler_params=pltpu.CompilerParams(
            collective_id=0, has_side_effects=True, vmem_limit_bytes=VMEM_LIMIT
        ),
        name="window",
    )(projected)

    spread = pieces * panels
    act, partial, bias_part = pl.pallas_call(
        spmm_kernel,
        out_shape=(
            jax.ShapeDtypeStruct((panels, side, width), BF),
            jax.ShapeDtypeStruct((spread, width, side), BF),
            jax.ShapeDtypeStruct((8, width), F32),
        ),
        in_specs=[smem(), smem(), smem(), vmem(), vmem(), vmem(), pl.BlockSpec(memory_space=pl.ANY)],
        out_specs=(vmem(), vmem(), vmem()),
        scratch_shapes=[
            pltpu.VMEM((slots, side, side), BF),
            pltpu.VMEM((panels + 1, side, width), F32),
            pltpu.VMEM((panels, width, side), BF),
            pltpu.VMEM((spread + 1, width, side), F32),
            pltpu.SemaphoreType.DMA((CHUNKS,)),
        ],
        compiler_params=pltpu.CompilerParams(vmem_limit_bytes=VMEM_LIMIT),
        name="sparse_products",
    )(
        block_counts, rows, cols,
        window.reshape(spread, side, width), bias.reshape(1, width),
        cotangent.reshape(panels, side, width), block_vals,
    )

    shared = width % (8 * n) == 0
    few = n if shared else 1
    step = width // n if shared else 8
    grad_feats, grad_weight, grad_bias = pl.pallas_call(
        functools.partial(reduce_kernel, n, shared),
        out_shape=(
            jax.ShapeDtypeStruct((panels, side, width_in), BF),
            jax.ShapeDtypeStruct((width_in, width), F32),
            jax.ShapeDtypeStruct((1, width), F32),
        ),
        in_specs=[vmem()] * 4,
        out_specs=(vmem(), vmem(), vmem()),
        scratch_shapes=[
            pltpu.VMEM((4, panels, width, side), BF),
            pltpu.VMEM((1, panels, width, side), BF),
            pltpu.VMEM((2, panels, width, side), BF),
            pltpu.VMEM((panels // 2, width, side), BF),
            pltpu.VMEM((panels // 2, width, side), BF),
            pltpu.VMEM((4, panels, width, side), BF),
            pltpu.VMEM((width, width_in), F32),
            pltpu.VMEM((few, step, width_in), F32),
            pltpu.VMEM((few, step, width_in), F32),
            pltpu.VMEM((few, 8, width), F32),
            pltpu.VMEM((8, width), F32),
            pltpu.SemaphoreType.DMA((16,)),
            pltpu.SemaphoreType.DMA((16,)),
            pltpu.SemaphoreType.DMA((3, few)),
            pltpu.SemaphoreType.DMA((3, few)),
        ],
        compiler_params=pltpu.CompilerParams(
            collective_id=1, has_side_effects=True, vmem_limit_bytes=VMEM_LIMIT
        ),
        name="reduce_back",
    )(
        partial.reshape(pieces, panels, width, side),
        nodes.reshape(panels, side, width_in), weight, bias_part,
    )
    grad_bias = grad_bias.reshape(width)
    if not shared:
        grad_weight, grad_bias = lax.psum((grad_weight, grad_bias), "blk")
    return (
        act.reshape(row_count, width),
        grad_feats.reshape(row_count, width_in),
        grad_weight,
        grad_bias,
    )


def solution(mesh):
    in_specs = (
        P(("grp", "blk"), None),
        P(("grp", "blk")),
        P(),
        P(),
        P(("grp", "blk"), None, None),
        P(("grp", "blk")),
        P(("grp", "blk")),
        P(("grp", "blk")),
        P(("grp", "blk"), None),
    )
    out_specs = (P(("grp", "blk"), None), P(("grp", "blk"), None), P("grp", None), P("grp"))
    return jax.shard_map(
        on_device, mesh=mesh, in_specs=in_specs, out_specs=out_specs, check_vma=False
    )
```

time: 521 us -> 150 us (0.29)
  waiting for transfers between devices: 171 us -> 0 us
  Pallas kernels: 0 us -> 143 us
  other arithmetic: 121 us -> 1.28 us
  blocking collectives: 72.6 us -> 0 us
  starting transfers between devices: 57 us -> 0 us
  local copies, waits for them, and re-layouts: 51.5 us -> 4.46 us
  matrix products: 31.2 us -> 0 us
  between operations: 14.8 us -> 1.32 us
    pallas_call x0 -> x4, Pallas kernels: none -> 143 us  [the longest x1 51.6 us: on_device(): pl.pallas_call(functools.partial(reduce_kernel, n, shared), out_shape=(ja...]
    scatter-add x2 -> x0, other arithmetic: 114 us -> none  [the longest x1 69.6 us: on_device(): jnp.zeros((spread, side, width), jnp.float32).at[local_cols].add(contrib)]
    ppermute x16 -> x0, waiting for transfers between devices: 89.8 us -> none  [passed_along(): lax.ppermute(shard, axis, [(i, (i + by) % length) for i in range(length)])]
    psum x1 -> x0, waiting for transfers between devices: 80.9 us -> none  [on_device(): grad_weight, grad_bias = lax.psum((weight_term, bias_term), 'blk')]
    psum x1 -> x0, blocking collectives: 72.6 us -> none  [on_device(): grad_weight, grad_bias = lax.psum((weight_term, bias_term), 'blk')]
    ppermute x16 -> x0, starting transfers between devices: 57 us -> none  [passed_along(): lax.ppermute(shard, axis, [(i, (i + by) % length) for i in range(length)])]
    dot_general x5 -> x0, matrix products: 31.2 us -> none  [the longest x1 14.2 us: on_device(): jnp.einsum('bij,bjh->bih', masked, window[local_cols], preferred_element_...]
    gather x3 -> x0, local copies, waits for them, and re-layouts: 30 us -> none  [the longest x1 13.1 us: on_device(): window[local_cols]]
  transfers between devices with their start and end apart: 17 -> 0, of which waited for: 6 -> 0; matrix products, arithmetic and copies ran while one was open for 2% -> 0% of each run, Pallas kernels for 0% -> 0%
where the time goes in v1:
time: 150 us
  Pallas kernels  143 us (95%)
  local copies, waits for them, and re-layouts  4.46 us (3%)
    pallas_call x1, Pallas kernels, on_device(): pl.pallas_call(functools.partial(reduce_kernel, n, shared), out_shape=(ja...  51.6 us
    pallas_call x1, Pallas kernels, on_device(): pl.pallas_call(spmm_kernel, out_shape=(jax.ShapeDtypeStruct((panels, side...  42.5 us
    pallas_call x1, Pallas kernels, on_device(): pl.pallas_call(functools.partial(window_kernel, n), out_shape=jax.ShapeDt...  40.8 us
    pallas_call x1, Pallas kernels, on_device(): pl.pallas_call(gather_kernel, out_shape=(jax.ShapeDtypeStruct((row_count,...  8.14 us
    unnamed x3, local copies, waits for them, and re-layouts  4.46 us

profile of v1, /device:TPU:0, one launch (start us, length us, event | category | flops | bytes accessed | tf_op | source)
XLA Modules:
  0.0 150.2 jit_solution(14270956932771276937)
XLA Ops:
  1.3 1.3 fusion.6
  2.6 8.1 %gather_project.1 = (bf16[2048,128]{1,0:T(8,128)(2,1)}, bf16[2048,128]{1,0:T(8,128)(2,1)}) custom-call(s32[2048]{0:T(1024)} %order.1, bf16[2048,128]{1,0:T(8,128)(2,1)} %feats.1, bf16[128,128]{1,0:T(8,128)(2,1)} %weight.3), custom_call_target="tpu_custom_call" | custom-call | tf_op jit(solution)/shard_map/gather_project/pallas_call | solution.py:409
  10.7 40.8 %window.1 = bf16[12,2048,128]{2,1,0:T(8,128)(2,1)} custom-call(bf16[2048,128]{1,0:T(8,128)(2,1)} %get-tuple-element.12.own), custom_call_target="tpu_custom_call" | custom-call | tf_op jit(solution)/shard_map/window/pallas_call | solution.py:425
  51.5 42.5 %sparse_products.1 = (bf16[16,128,128]{2,1,0:T(8,128)(2,1)}, bf16[192,128,128]{2,1,0:T(8,128)(2,1)}, f32[8,128]{1,0:T(8,128)}) custom-call(s32[1]{0:T(128)S(6)} %copy.16.counts, s32[336]{0:T(512)} %get-tuple-element.21.rows, s32[336]{0:T(512)} %get-tuple-element.20.cols, bf16[192,128,128]{2,1,0:T(8,128)(2,1)} %bitcast.8, f32[1,128]{1,0:T(1,128)} %bitcast.13, ...), custom_call_target="tpu_custom_call" | custom-call | tf_op jit(solution)/shard_map/sparse_products/pallas_call | solution.py:442
  94.1 51.6 %reduce_back.1 = (bf16[16,128,128]{2,1,0:T(8,128)(2,1)}, f32[128,128]{1,0:T(8,128)}, f32[1,128]{1,0:T(1,128)}) custom-call(bf16[12,16,128,128]{3,2,1,0:T(8,128)(2,1)} %bitcast.9, bf16[16,128,128]{2,1,0:T(8,128)(2,1)} %bitcast.11, bf16[128,128]{1,0:T(8,128)(2,1)} %weight.3, f32[8,128]{1,0:T(8,128)} %get-tuple-element.16.grad_bias), custom_call_target="tpu_custom_call" | custom-call | tf_op jit(solution)/shard_map/reduce_back/pallas_call | solution.py:469
  145.7 1.9 %copy.17 = bf16[2048,128]{1,0:T(8,128)(2,1)} copy(bf16[2048,128]{1,0:T(8,128)(2,1)} %bitcast.12) | data formatting | bytes 1048576
  147.6 1.5 copy.18
  149.0 1.1 copy.19

commit v2 on v1

--- a/solution.py
+++ b/solution.py
@@ -8,8 +8,10 @@
 from jax.sharding import PartitionSpec as P
 
 QUAD = 4
-CHUNKS = 12
-UNROLL = 4
+CHUNKS = 7
+UNROLL = 16
+PARTS = 8
+RELAYED = 0
 BF = jnp.bfloat16
 F32 = jnp.float32
 MESH = pl.DeviceIdType.MESH
@@ -20,19 +22,24 @@
     return pl.BlockSpec(memory_space=pltpu.VMEM)
 
 
+def anywhere():
+    return pl.BlockSpec(memory_space=pl.ANY)
+
+
 def smem():
     return pl.BlockSpec(memory_space=pltpu.SMEM)
 
 
 def gather_kernel(order, feats, weight, nodes, projected, wide, picked):
     count = feats.shape[0]
+    first = lax.axis_index("blk") * count
     wide[...] = feats[...].astype(F32)
 
     def body(i, carry):
         base = pl.multiple_of(i * 16, 16)
+        taken = [wide[pl.ds(order[base + u] - first, 1), :] for u in range(16)]
         for u in range(16):
-            src = lax.rem(order[base + u], count)
-            picked[pl.ds(base + u, 1), :] = wide[pl.ds(src, 1), :]
+            picked[pl.ds(base + u, 1), :] = taken[u]
         return carry
 
     lax.fori_loop(0, count // 16, body, 0)
@@ -88,7 +95,7 @@
     tj = y * 2 + (1 - c)
     fj = (1 - y) * 2 + (1 - c)
     beyond = (1 - y) * up + y * down
-    half = own.shape[0] // 2
+    half = own.shape[0] // PARTS
     greet((up, down, across, twin))
     sent = []
 
@@ -113,34 +120,37 @@
         ).wait_recv()
         return spot
 
-    for h in (1, 0):
-        mine = own.at[pl.ds(h * half, half), :]
-        push(mine, 1, j, h, across)
-        push(mine, 0, j, h, up)
-        push(mine, 2, j, h, down)
-        push(mine, 1, j, h, twin)
+    def mine(h):
+        return own.at[pl.ds(h * half, half), :]
+
+    direct = PARTS - RELAYED
+    near, other = 2 * (1 - y), 2 * y
+    zs, zo = 2 * (1 - c), 2 * c
+    for i in range(PARTS):
+        push(mine(PARTS - 1 - i), 1, j, PARTS - 1 - i, across)
+        push(mine(i), 0, j, i, up)
+        push(mine(i), 2, j, i, down)
+    for h in range(PARTS):
+        push(mine(h), 1, j, h, twin)
     keep = pltpu.make_async_copy(own, window.at[QUAD + j], local_sem)
     keep.start()
-
-    spot = arrived(1, nj, 1)
-    push(spot, 2 * y, nj, 1, beyond)
-    push(spot, 1, nj, 1, twin)
-    near, other = 2 * (1 - y), 2 * y
-    zs = 2 * (1 - c)
-    zo = 2 * c
-    for h in (1, 0):
-        if h == 0:
-            spot = arrived(1, nj, 0)
-            push(spot, 1, nj, 0, twin)
-        spot = arrived(near, j, h)
-        if h == 0:
-            push(spot, near, j, 0, across)
-        arrived(other, j, h)
-        push(piece(zs, j, h), zs, j, h, twin)
-    for h in (1, 0):
-        spot = arrived(2 * y, nj, h)
-        push(spot, 2 * y, nj, h, twin)
-    for h in (1, 0):
+    for i in range(PARTS):
+        h = PARTS - 1 - i
+        spot = arrived(1, nj, h)
+        if h >= direct:
+            push(spot, 2 * y, nj, h, beyond)
+        push(spot, 1, nj, h, twin)
+        spot = arrived(near, j, i)
+        if i < direct:
+            push(spot, near, j, i, across)
+        arrived(other, j, i)
+        push(piece(zs, j, i), zs, j, i, twin)
+    far = []
+    for i in range(PARTS):
+        far += [h for h in (PARTS - 1 - i, i) if h not in far]
+    for h in far:
+        push(arrived(2 * y, nj, h), 2 * y, nj, h, twin)
+    for h in range(PARTS):
         arrived(1, tj, h)
         arrived(1, fj, h)
         arrived(zo, tj, h)
@@ -151,14 +161,27 @@
 
 
 def spmm_kernel(
-    counts, rows, cols, window, bias, cotangent, vals_hbm,
-    act, partial, grad_bias, vals, acc, flipped, grads, sems,
+    n, counts, block_rows, block_cols, window_hbm, bias, cotangent, vals_hbm,
+    act, partial, grad_bias, vals, window, acc, flipped, grads, sems, window_sem,
 ):
     slots, side, width = vals_hbm.shape
     panels = acc.shape[0] - 1
     spread = grads.shape[0] - 1
     per = slots // CHUNKS
     count = counts[0]
+    me = lax.axis_index("blk")
+    quads = n // QUAD
+    first_row = me * panels
+    first_col = lax.rem(me // QUAD + quads - 1, quads) * (QUAD * panels)
+    fill = pltpu.make_async_copy(window_hbm, window, window_sem)
+    fill.start()
+
+    def row_of(s):
+        return block_rows[s] - first_row
+
+    def col_of(s):
+        away = block_cols[s] - first_col
+        return jnp.where(away < 0, away + n * panels, away)
 
     def fetch(k):
         at = pl.ds(k * per, per)
@@ -171,13 +194,20 @@
 
     acc[...] = jnp.zeros_like(acc)
 
+    def clear(p, carry):
+        grads[p] = jnp.zeros((side, width), F32)
+        return carry
+
+    lax.fori_loop(0, spread, clear, 0)
+    fill.wait()
+
     def forward(i, carry):
         at = [i * UNROLL + u for u in range(UNROLL)]
         prods = [
-            jnp.dot(vals[s], window[cols[s]], preferred_element_type=F32) for s in at
+            jnp.dot(vals[s], window[col_of(s)], preferred_element_type=F32) for s in at
         ]
         for s, prod in zip(at, prods):
-            row = jnp.where(s < count, rows[s], panels)
+            row = jnp.where(s < count, row_of(s), panels)
             acc[row] += prod
         return carry
 
@@ -186,12 +216,6 @@
         def _(k=k):
             fetch(k).wait()
             lax.fori_loop(k * per // UNROLL, (k + 1) * per // UNROLL, forward, 0)
-
-    def clear(p, carry):
-        grads[p] = jnp.zeros((side, width), F32)
-        return carry
-
-    lax.fori_loop(0, spread, clear, 0)
 
     def middle(r, total):
         mixed = acc[r] + bias[...]
@@ -207,10 +231,10 @@
     def backward(i, carry):
         at = [i * UNROLL + u for u in range(UNROLL)]
         prods = [
-            jnp.dot(flipped[rows[s]], vals[s], preferred_element_type=F32) for s in at
+            jnp.dot(flipped[row_of(s)], vals[s], preferred_element_type=F32) for s in at
         ]
         for s, prod in zip(at, prods):
-            col = jnp.where(s < count, cols[s], spread)
+            col = jnp.where(s < count, col_of(s), spread)
             grads[col] += prod
         return carry
 
@@ -226,7 +250,7 @@
 def reduce_kernel(
     n, shared, partial, nodes, weight, grad_bias,
     grad_feats, grad_weight, bias_out,
-    from_twin, from_across, from_z, far_across, far_z, mid, work,
+    from_twin, from_across, from_z, far, mid, work,
     share, gathered, biases, own_bias,
     send_sem, recv_sem, small_send, small_recv,
 ):
@@ -235,7 +259,8 @@
     tj = y * 2 + (1 - c)
     fj = (1 - y) * 2 + (1 - c)
     panels = partial.shape[1]
-    half = panels // 2
+    half = panels // PARTS
+    direct = PARTS - RELAYED
     if shared:
         greet([(me + d) % n for d in range(1, n)])
     else:
@@ -273,9 +298,12 @@
         (2, 2 * c * QUAD + tj),
         (3, QUAD + tj),
     ]
+    turns = []
+    for i in range(PARTS):
+        turns += [h for h in (PARTS - 1 - i, i) if h not in turns]
     for k, index in order:
-        for h in (1, 0):
-            push(part(partial, index, h), part(from_twin, k, h), 2 * k + h, twin)
+        for h in turns:
+            push(part(partial, index, h), part(from_twin, k, h), k * PARTS + h, twin)
     if shared:
         small = []
         own_bias[...] = grad_bias[...]
@@ -287,49 +315,57 @@
         biases[me] = grad_bias[...]
 
     back = (1 - y) * down + y * up
-    for h in (1, 0):
+    for h in turns:
         arrived(part(from_twin, 0, h), h)
         merge(part(mid, 0, h), part(partial, 2 * y * QUAD + nj, h), part(from_twin, 0, h))
-        if h == 1:
-            push(part(mid, 0, 1), far_z, 8, back)
-        else:
-            push(part(mid, 0, 0), far_across, 9, across)
-    near, other = 2 * (1 - y), 2 * y
+        push(part(mid, 0, h), part(far, 0, h), 4 * PARTS + h, across if h < direct else back)
+    near = 2 * (1 - y)
     zs, zo = 2 * (1 - c), 2 * c
-    for h in (1, 0):
-        arrived(part(from_twin, 2, h), 4 + h)
-        merge(part(mid, 2, h), part(partial, zs * QUAD + j, h), part(from_twin, 2, h))
-
-        def fill(p, carry, h=h):
-            mid[1, h * half + p] = partial[zo * QUAD + j, h * half + p]
-            return carry
-
-        lax.fori_loop(0, half, fill, 0)
     near_at = 1 + (near == zs).astype(jnp.int32)
     zs_up = (zs == 2).astype(jnp.int32)
     to_zs = zs_up * up + (1 - zs_up) * down
     to_zo = (1 - zs_up) * up + zs_up * down
-    push(part(mid, 2, 1), part(from_z, 1 - zs_up, 1), 10 + 2 * (1 - zs_up) + 1, to_zs)
-    push(part(mid, 1, 1), part(from_z, zs_up, 1), 10 + 2 * zs_up + 1, to_zo)
-    arrived(far_across, 9)
-    merge(part(mid, near_at, 0), part(mid, near_at, 0), far_across)
-    push(part(mid, 2, 0), part(from_z, 1 - zs_up, 0), 10 + 2 * (1 - zs_up), to_zs)
-    push(part(mid, 1, 0), part(from_z, zs_up, 0), 10 + 2 * zs_up, to_zo)
-    arrived(part(from_twin, 1, 0), 2)
-    merge(part(mid, 3, 0), part(partial, QUAD + nj, 0), part(from_twin, 1, 0))
-    push(part(mid, 3, 0), part(from_across, 0, 0), 14, across)
-    arrived(part(from_twin, 1, 1), 3)
-    merge(part(mid, 3, 1), part(partial, QUAD + nj, 1), part(from_twin, 1, 1))
-    arrived(far_z, 8)
-    merge(part(mid, 3, 1), part(mid, 3, 1), far_z)
-    push(part(mid, 3, 1), part(from_across, 0, 1), 15, across)
+
+    def beside(h, joined):
+        arrived(part(from_twin, 2, h), 2 * PARTS + h)
+        merge(part(mid, 2, h), part(partial, zs * QUAD + j, h), part(from_twin, 2, h))
+
+        def fill(p, carry):
+            mid[1, h * half + p] = partial[zo * QUAD + j, h * half + p]
+            return carry
+
+        lax.fori_loop(0, half, fill, 0)
+        if joined:
+            arrived(part(far, 0, h), 4 * PARTS + h)
+            merge(part(mid, near_at, h), part(mid, near_at, h), part(far, 0, h))
+        push(part(mid, 2, h), part(from_z, 1 - zs_up, h), (6 - zs_up) * PARTS + h, to_zs)
+        push(part(mid, 1, h), part(from_z, zs_up, h), (5 + zs_up) * PARTS + h, to_zo)
+
+    def over(h, joined):
+        arrived(part(from_twin, 1, h), PARTS + h)
+        merge(part(mid, 3, h), part(partial, QUAD + nj, h), part(from_twin, 1, h))
+        if joined:
+            arrived(part(far, 0, h), 4 * PARTS + h)
+            merge(part(mid, 3, h), part(mid, 3, h), part(far, 0, h))
+        push(part(mid, 3, h), part(from_across, 0, h), 7 * PARTS + h, across)
+
+    for h in turns:
+        if h < direct:
+            over(h, False)
+        else:
+            beside(h, False)
+    for h in turns:
+        if h < direct:
+            beside(h, True)
+        else:
+            over(h, True)
 
     work[...] = jnp.zeros_like(work)
-    for h in (0, 1):
-        arrived(part(from_twin, 3, h), 6 + h)
-        arrived(part(from_z, 0, h), 10 + h)
-        arrived(part(from_z, 1, h), 12 + h)
-        arrived(part(from_across, 0, h), 14 + h)
+    for h in turns:
+        arrived(part(from_twin, 3, h), 3 * PARTS + h)
+        arrived(part(from_z, 0, h), 5 * PARTS + h)
+        arrived(part(from_z, 1, h), 6 * PARTS + h)
+        arrived(part(from_across, 0, h), 7 * PARTS + h)
 
         def finish(i, carry, h=h):
             p = h * half + i
@@ -397,14 +433,7 @@
     width = weight.shape[1]
     panels = row_count // side
     n = lax.axis_size("blk")
-    quads = n // QUAD
     pieces = 3 * QUAD
-    me = lax.axis_index("blk")
-
-    rows = block_rows - me * panels
-    owner = block_cols // panels
-    slot = jnp.mod(owner // QUAD - me // QUAD + 1 + quads, quads)
-    cols = (slot * QUAD + owner % QUAD) * panels + block_cols % panels
 
     nodes, projected = pl.pallas_call(
         gather_kernel,
@@ -426,10 +455,10 @@
         functools.partial(window_kernel, n),
         out_shape=jax.ShapeDtypeStruct((pieces, row_count, width), BF),
         in_specs=[vmem()],
-        out_specs=vmem(),
+        out_specs=anywhere(),
         scratch_shapes=[
-            pltpu.SemaphoreType.DMA((24,)),
-            pltpu.SemaphoreType.DMA((pieces, 2)),
+            pltpu.SemaphoreType.DMA((8 * PARTS,)),
+            pltpu.SemaphoreType.DMA((pieces, PARTS)),
             pltpu.SemaphoreType.DMA,
         ],
         compiler_params=pltpu.CompilerParams(
@@ -440,25 +469,27 @@
 
     spread = pieces * panels
     act, partial, bias_part = pl.pallas_call(
-        spmm_kernel,
+        functools.partial(spmm_kernel, n),
         out_shape=(
             jax.ShapeDtypeStruct((panels, side, width), BF),
             jax.ShapeDtypeStruct((spread, width, side), BF),
             jax.ShapeDtypeStruct((8, width), F32),
         ),
-        in_specs=[smem(), smem(), smem(), vmem(), vmem(), vmem(), pl.BlockSpec(memory_space=pl.ANY)],
+        in_specs=[smem(), smem(), smem(), anywhere(), vmem(), vmem(), anywhere()],
         out_specs=(vmem(), vmem(), vmem()),
         scratch_shapes=[
             pltpu.VMEM((slots, side, side), BF),
+            pltpu.VMEM((spread, side, width), BF),
             pltpu.VMEM((panels + 1, side, width), F32),
             pltpu.VMEM((panels, width, side), BF),
             pltpu.VMEM((spread + 1, width, side), F32),
             pltpu.SemaphoreType.DMA((CHUNKS,)),
+            pltpu.SemaphoreType.DMA,
         ],
         compiler_params=pltpu.CompilerParams(vmem_limit_bytes=VMEM_LIMIT),
         name="sparse_products",
     )(
-        block_counts, rows, cols,
+        block_counts, block_rows, block_cols,
         window.reshape(spread, side, width), bias.reshape(1, width),
         cotangent.reshape(panels, side, width), block_vals,
     )
@@ -479,16 +510,15 @@
             pltpu.VMEM((4, panels, width, side), BF),
             pltpu.VMEM((1, panels, width, side), BF),
             pltpu.VMEM((2, panels, width, side), BF),
-            pltpu.VMEM((panels // 2, width, side), BF),
-            pltpu.VMEM((panels // 2, width, side), BF),
+            pltpu.VMEM((1, panels, width, side), BF),
             pltpu.VMEM((4, panels, width, side), BF),
             pltpu.VMEM((width, width_in), F32),
             pltpu.VMEM((few, step, width_in), F32),
             pltpu.VMEM((few, step, width_in), F32),
             pltpu.VMEM((few, 8, width), F32),
             pltpu.VMEM((8, width), F32),
-            pltpu.SemaphoreType.DMA((16,)),
-            pltpu.SemaphoreType.DMA((16,)),
+            pltpu.SemaphoreType.DMA((8 * PARTS,)),
+            pltpu.SemaphoreType.DMA((8 * PARTS,)),
             pltpu.SemaphoreType.DMA((3, few)),
             pltpu.SemaphoreType.DMA((3, few)),
         ],

time: 150 us -> 120 us (0.80)
  Pallas kernels: 143 us -> 113 us
    pallas_call x1, Pallas kernels: 42.5 us -> 21.3 us  [on_device(): pl.pallas_call(functools.partial(spmm_kernel, n), out_shape=(jax.ShapeDty...]
    pallas_call x1, Pallas kernels: 40.8 us -> 36.7 us  [on_device(): pl.pallas_call(functools.partial(window_kernel, n), out_shape=jax.ShapeDt...]
    pallas_call x1, Pallas kernels: 8.14 us -> 5.46 us  [on_device(): pl.pallas_call(gather_kernel, out_shape=(jax.ShapeDtypeStruct((row_count,...]
    pallas_call x1, Pallas kernels: 51.6 us -> 50 us  [on_device(): pl.pallas_call(functools.partial(reduce_kernel, n, shared), out_shape=(ja...]
where the time goes in v2:
time: 120 us; the launch traced here: 119 us
  Pallas kernels  113 us (94%)
  local copies, waits for them, and re-layouts  4.48 us (4%)
  between operations  1.3 us (1%)
    pallas_call x1, Pallas kernels, on_device(): pl.pallas_call(functools.partial(reduce_kernel, n, shared), out_shape=(ja...  50 us
    pallas_call x1, Pallas kernels, on_device(): pl.pallas_call(functools.partial(window_kernel, n), out_shape=jax.ShapeDt...  36.7 us
    pallas_call x1, Pallas kernels, on_device(): pl.pallas_call(functools.partial(spmm_kernel, n), out_shape=(jax.ShapeDty...  21.3 us
    pallas_call x1, Pallas kernels, on_device(): pl.pallas_call(gather_kernel, out_shape=(jax.ShapeDtypeStruct((row_count,...  5.46 us
    unnamed x3, local copies, waits for them, and re-layouts  4.48 us

profile of v2, /device:TPU:0, one launch (start us, length us, event | category | flops | bytes accessed | tf_op | source)
XLA Modules:
  0.0 119.1 jit_solution(12373599884740244256)
XLA Ops:
  1.3 5.5 %gather_project.1 = (bf16[2048,128]{1,0:T(8,128)(2,1)}, bf16[2048,128]{1,0:T(8,128)(2,1)}) custom-call(s32[2048]{0:T(1024)} %order.1, bf16[2048,128]{1,0:T(8,128)(2,1)} %feats.1, bf16[128,128]{1,0:T(8,128)(2,1)} %weight.3), custom_call_target="tpu_custom_call" | custom-call | tf_op jit(solution)/shard_map/gather_project/pallas_call | solution.py:438
  6.7 36.7 %window.1 = bf16[12,2048,128]{2,1,0:T(8,128)(2,1)} custom-call(bf16[2048,128]{1,0:T(8,128)(2,1)} %get-tuple-element.12.own), custom_call_target="tpu_custom_call" | custom-call | tf_op jit(solution)/shard_map/window/pallas_call | solution.py:454
  43.4 21.3 %sparse_products.1 = (bf16[16,128,128]{2,1,0:T(8,128)(2,1)}, bf16[192,128,128]{2,1,0:T(8,128)(2,1)}, f32[8,128]{1,0:T(8,128)}) custom-call(s32[1]{0:T(128)S(6)} %copy.16.counts, s32[336]{0:T(512)} %block_rows.1, s32[336]{0:T(512)} %block_cols.1, bf16[192,128,128]{2,1,0:T(8,128)(2,1)} %bitcast.8, f32[1,128]{1,0:T(1,128)} %bitcast.13, ...), custom_call_target="tpu_custom_call" | custom-call | tf_op jit(solution)/shard_map/sparse_products/pallas_call | solution.py:471
  64.7 50.0 %reduce_back.1 = (bf16[16,128,128]{2,1,0:T(8,128)(2,1)}, f32[128,128]{1,0:T(8,128)}, f32[1,128]{1,0:T(1,128)}) custom-call(bf16[12,16,128,128]{3,2,1,0:T(8,128)(2,1)} %bitcast.9, bf16[16,128,128]{2,1,0:T(8,128)(2,1)} %bitcast.11, bf16[128,128]{1,0:T(8,128)(2,1)} %weight.3, f32[8,128]{1,0:T(8,128)} %get-tuple-element.16.grad_bias), custom_call_target="tpu_custom_call" | custom-call | tf_op jit(solution)/shard_map/reduce_back/pallas_call | solution.py:500
  114.6 1.9 %copy.17 = bf16[2048,128]{1,0:T(8,128)(2,1)} copy(bf16[2048,128]{1,0:T(8,128)(2,1)} %bitcast.12) | data formatting | bytes 1048576
  116.5 1.5 %copy.18 = f32[128,128]{1,0:T(8,128)} copy(f32[128,128]{1,0:T(8,128)} %get-tuple-element.26) | data formatting | bytes 131072
  118.0 1.1 copy.19

commit v3 on v2

--- a/solution.py
+++ b/solution.py
@@ -9,8 +9,8 @@
 
 QUAD = 4
 CHUNKS = 7
-UNROLL = 16
-PARTS = 8
+UNROLL = 24
+PARTS = 4
 RELAYED = 0
 BF = jnp.bfloat16
 F32 = jnp.float32
@@ -36,13 +36,13 @@
     wide[...] = feats[...].astype(F32)
 
     def body(i, carry):
-        base = pl.multiple_of(i * 16, 16)
-        taken = [wide[pl.ds(order[base + u] - first, 1), :] for u in range(16)]
-        for u in range(16):
+        base = pl.multiple_of(i * 32, 32)
+        taken = [wide[pl.ds(order[base + u] - first, 1), :] for u in range(32)]
+        for u in range(32):
             picked[pl.ds(base + u, 1), :] = taken[u]
         return carry
 
-    lax.fori_loop(0, count // 16, body, 0)
+    lax.fori_loop(0, count // 32, body, 0)
     part = 512 if count % 512 == 0 else count
 
     def product(i, carry):
@@ -52,7 +52,7 @@
         projected[at, :] = jnp.dot(rows, weight[...], preferred_element_type=F32).astype(BF)
         return carry
 
-    lax.fori_loop(0, count // part, product, 0)
+    lax.fori_loop(0, count // part, product, 0, unroll=True)
 
 
 def places(n):
@@ -198,7 +198,7 @@
         grads[p] = jnp.zeros((side, width), F32)
         return carry
 
-    lax.fori_loop(0, spread, clear, 0)
+    lax.fori_loop(0, spread, clear, 0, unroll=4)
     fill.wait()
 
     def forward(i, carry):
@@ -226,7 +226,7 @@
         flipped[r] = low.T.astype(BF)
         return total + jnp.sum(low.reshape(side // 8, 8, width), axis=0)
 
-    grad_bias[...] = lax.fori_loop(0, panels, middle, jnp.zeros((8, width), F32))
+    grad_bias[...] = lax.fori_loop(0, panels, middle, jnp.zeros((8, width), F32), unroll=4)
 
     def backward(i, carry):
         at = [i * UNROLL + u for u in range(UNROLL)]
@@ -244,7 +244,7 @@
         partial[p] = grads[p].astype(BF)
         return carry
 
-    lax.fori_loop(0, spread, store, 0)
+    lax.fori_loop(0, spread, store, 0, unroll=4)
 
 
 def reduce_kernel(
@@ -290,7 +290,7 @@
             dst[p] = (a[p].astype(F32) + b[p].astype(F32)).astype(BF)
             return carry
 
-        lax.fori_loop(0, half, body, 0)
+        lax.fori_loop(0, half, body, 0, unroll=True)
 
     order = [
         (0, 2 * y * QUAD + fj),
@@ -334,7 +334,7 @@
             mid[1, h * half + p] = partial[zo * QUAD + j, h * half + p]
             return carry
 
-        lax.fori_loop(0, half, fill, 0)
+        lax.fori_loop(0, half, fill, 0, unroll=True)
         if joined:
             arrived(part(far, 0, h), 4 * PARTS + h)
             merge(part(mid, near_at, h), part(mid, near_at, h), part(far, 0, h))
@@ -380,7 +380,7 @@
             ).astype(BF)
             return carry
 
-        lax.fori_loop(0, half, finish, 0)
+        lax.fori_loop(0, half, finish, 0, unroll=True)
 
     if shared:
         step = work.shape[0] // n

time: 120 us -> 114 us (0.950); the launches traced: 119 us -> 114 us
  Pallas kernels: 113 us -> 109 us
    pallas_call x1, Pallas kernels: 50 us -> 46.6 us  [on_device(): pl.pallas_call(functools.partial(reduce_kernel, n, shared), out_shape=(ja...]
    pallas_call x1, Pallas kernels: 36.7 us -> 35.4 us  [on_device(): pl.pallas_call(functools.partial(window_kernel, n), out_shape=jax.ShapeDt...]
where the time goes in v3:
time: 114 us
  Pallas kernels  109 us (96%)
  local copies, waits for them, and re-layouts  4.48 us (4%)
  between operations  1.3 us (1%)
    pallas_call x1, Pallas kernels, on_device(): pl.pallas_call(functools.partial(reduce_kernel, n, shared), out_shape=(ja...  46.6 us
    pallas_call x1, Pallas kernels, on_device(): pl.pallas_call(functools.partial(window_kernel, n), out_shape=jax.ShapeDt...  35.4 us
    pallas_call x1, Pallas kernels, on_device(): pl.pallas_call(functools.partial(spmm_kernel, n), out_shape=(jax.ShapeDty...  21.9 us
    pallas_call x1, Pallas kernels, on_device(): pl.pallas_call(gather_kernel, out_shape=(jax.ShapeDtypeStruct((row_count,...  4.59 us
    unnamed x3, local copies, waits for them, and re-layouts  4.48 us

profile of v3, /device:TPU:0, one launch (start us, length us, event | category | flops | bytes accessed | tf_op | source)
XLA Modules:
  0.0 114.3 jit_solution(5133648208366070579)
XLA Ops:
  1.3 4.6 %gather_project.1 = (bf16[2048,128]{1,0:T(8,128)(2,1)}, bf16[2048,128]{1,0:T(8,128)(2,1)}) custom-call(s32[2048]{0:T(1024)} %order.1, bf16[2048,128]{1,0:T(8,128)(2,1)} %feats.1, bf16[128,128]{1,0:T(8,128)(2,1)} %weight.3), custom_call_target="tpu_custom_call" | custom-call | tf_op jit(solution)/shard_map/gather_project/pallas_call | solution.py:438
  5.9 35.4 %window.1 = bf16[12,2048,128]{2,1,0:T(8,128)(2,1)} custom-call(bf16[2048,128]{1,0:T(8,128)(2,1)} %get-tuple-element.12.own), custom_call_target="tpu_custom_call" | custom-call | tf_op jit(solution)/shard_map/window/pallas_call | solution.py:454
  41.3 21.9 %sparse_products.1 = (bf16[16,128,128]{2,1,0:T(8,128)(2,1)}, bf16[192,128,128]{2,1,0:T(8,128)(2,1)}, f32[8,128]{1,0:T(8,128)}) custom-call(s32[1]{0:T(128)S(6)} %copy.16.counts, s32[336]{0:T(512)} %block_rows.1, s32[336]{0:T(512)} %block_cols.1, bf16[192,128,128]{2,1,0:T(8,128)(2,1)} %bitcast.8, f32[1,128]{1,0:T(1,128)} %bitcast.13, ...), custom_call_target="tpu_custom_call" | custom-call | tf_op jit(solution)/shard_map/sparse_products/pallas_call | solution.py:471
  63.2 46.6 %reduce_back.1 = (bf16[16,128,128]{2,1,0:T(8,128)(2,1)}, f32[128,128]{1,0:T(8,128)}, f32[1,128]{1,0:T(1,128)}) custom-call(bf16[12,16,128,128]{3,2,1,0:T(8,128)(2,1)} %bitcast.9, bf16[16,128,128]{2,1,0:T(8,128)(2,1)} %bitcast.11, bf16[128,128]{1,0:T(8,128)(2,1)} %weight.3, f32[8,128]{1,0:T(8,128)} %get-tuple-element.16.grad_bias), custom_call_target="tpu_custom_call" | custom-call | tf_op jit(solution)/shard_map/reduce_back/pallas_call | solution.py:500
  109.8 1.9 %copy.17 = bf16[2048,128]{1,0:T(8,128)(2,1)} copy(bf16[2048,128]{1,0:T(8,128)(2,1)} %bitcast.12) | data formatting | bytes 1048576
  111.7 1.5 %copy.18 = f32[128,128]{1,0:T(8,128)} copy(f32[128,128]{1,0:T(8,128)} %get-tuple-element.26) | data formatting | bytes 131072
  113.2 1.1 copy.19
